TPU v7x, 32 devices: a whole 2x2x4 slice. The times are simulated.
32 devices in a mesh: zone: 8 (over z, y), var: 4 (over x, core).
Axes of the slice: x: 2, y: 2, z: 4, core: 2. Of those that a mesh axis runs over, the one named last changes fastest.
Arguments:
- history: float32 [48, 64, 4096], P('var', None, 'zone'), may hold values from -6 to 6
- adjacency: int32 [6, 4096], P(None, 'zone'), may hold values from -1 to 4095, as said below
- volume_op: float32 [64, 64], replicated, may hold values from -0.375 to 0.375
- face_lift: float32 [6, 64, 64], replicated, may hold values from -0.1875 to 0.1875
- schmid_map: float32 [48, 12], replicated, may hold values from -0.875 to 0.875
- hardening: float32 [12, 48], replicated, may hold values from -1.75 to 1.75
Outputs:
- remapped: float32 [48, 64, 4096], P('var', None, 'zone')
Inputs may be any that keep to these rules, and one draw needn't show every extreme that they name: `adjacency`: every entry is -1 or a zone whose index differs from the zone's own by at most 64; differences of exactly 64 and -64 occur.
All inputs are finite; a program needn't handle non-finite values.
Results may differ from a plain program's by a relative error of at most 0.0001.
Values sent between devices are 32-bit elements; how exact they have to be, the bound alone decides.
A program may use at most 128 MiB of HBM per device.

v0:
```python
import jax
import jax.numpy as jnp
from jax import lax
from jax.sharding import PartitionSpec as P


def padded(block, sides, width):
    for axis, dim in sides:
        count = lax.axis_size(axis)
        forward = [(i, i + 1) for i in range(count - 1)]
        backward = [(target, source) for source, target in forward]
        low = lax.ppermute(
            lax.slice_in_dim(block, block.shape[dim] - width, None, axis=dim), axis, forward
        )
        high = lax.ppermute(lax.slice_in_dim(block, 0, width, axis=dim), axis, backward)
        block = jnp.concatenate([low, block, high], axis=dim)
    return block


def advect_operator(field, adjacency, volume_op, face_lift, offset):
    rim = field.shape[2] // 8
    extended = padded(field, (("zone", 2),), rim)
    result = jnp.einsum("vrz,rp->vpz", field, volume_op, precision=lax.Precision.HIGHEST)
    for face in range(6):
        face_index = adjacency[face]
        local_index = jnp.where(face_index >= 0, face_index - offset + rim, 0)
        neighbour = jnp.take(extended, local_index, axis=2)
        neighbour = jnp.where(face_index[None, None, :] >= 0, neighbour, jnp.float32(0.0))
        result = result + jnp.einsum(
            "vrz,rp->vpz", neighbour, face_lift[face], precision=lax.Precision.HIGHEST
        )
    return result


def point_update(points, schmid_map, hardening, stride):
    shear = jnp.einsum("va,vpz->apz", schmid_map, points, precision=lax.Precision.HIGHEST)
    updated = points + jnp.einsum(
        "av,apz->vpz", hardening, jnp.tanh(shear), precision=lax.Precision.HIGHEST
    )
    rotation = updated[0 : 4 * stride : stride]
    length = jnp.sqrt(jnp.sum(rotation * rotation, axis=0))
    factor = 1.0 / jnp.maximum(length, 1.0)
    return updated.at[0 : 4 * stride : stride].multiply(factor[None])


def per_device(history, adjacency, volume_op, face_lift, schmid_map, hardening):
    local_vars = history.shape[0]
    local_zones = history.shape[2]
    offset = lax.axis_index("zone") * local_zones
    section_one = history + advect_operator(history, adjacency, volume_op, face_lift, offset)
    section_two = 0.75 * history + 0.25 * (
        section_one + advect_operator(section_one, adjacency, volume_op, face_lift, offset)
    )
    advected = history / 3.0 + 2.0 / 3.0 * (
        section_two + advect_operator(section_two, adjacency, volume_op, face_lift, offset)
    )
    points = lax.all_to_all(advected, "var", split_axis=2, concat_axis=0, tiled=True)
    renewed = point_update(points, schmid_map, hardening, local_vars)
    return lax.all_to_all(renewed, "var", split_axis=0, concat_axis=2, tiled=True)


def solution(mesh):
    in_specs = (P("var", None, "zone"), P(None, "zone"), P(), P(), P(), P())
    out_specs = P("var", None, "zone")
    return jax.shard_map(
        per_device, mesh=mesh, in_specs=in_specs, out_specs=out_specs, check_vma=False
    )
```

profile of v0, /device:TPU:16, one launch (start us, length us, event | category | flops | bytes accessed | tf_op | source)
XLA Modules:
  0.0 423.3 jit_solution(7639713367770886351)
XLA Ops:
  14.0 8.8 %collective-permute-done = f32[12,64,64]{2,1,0:T(8,128)} collective-permute-done((f32[12,64,64]{2,1,0:T(8,128)}, f32[12,64,64]{2,1,0:T(8,128)}, u32[]{:S(2)}, u32[]{:S(2)}) %collective-permute-start) | collective-permute-done | bytes 196640 | tf_op jit(solution)/shard_map/ppermute | solution.py:12
  27.7 6.2 %copy.161 = f32[12,64,640]{1,0,2:T(8,128)} copy(f32[12,64,640]{2,1,0:T(8,128)} %pad_maximum_fusion) | data formatting | bytes 3932160 | tf_op jit(solution)/shard_map/concatenate | solution.py:16
  33.9 5.6 %gather_fusion.3 = f32[512,12,64]{2,1,0:T(8,128)} fusion(f32[12,64,640]{1,0,2:T(8,128)} %copy.161, s32[1024]{0:T(1024)S(1)} %pad_clamp_fusion.2), kind=kCustom, calls=%fused_computation.3.clone | custom fusion | bytes 3147776 | tf_op jit(solution)/shard_map/jit(_take)/gather | solution.py:27
  39.5 5.5 %gather_fusion.2 = f32[512,12,64]{2,1,0:T(8,128)} fusion(f32[12,64,640]{1,0,2:T(8,128)} %copy.161, s32[1024]{0:T(1024)S(1)} %pad_clamp_fusion.3), kind=kCustom, calls=%fused_computation.2.clone | custom fusion | bytes 3147776 | tf_op jit(solution)/shard_map/jit(_take)/gather | solution.py:27
  50.1 5.8 %fusion.28 = f32[12,512,64]{1,2,0:T(8,128)} fusion(f32[12,64,512]{1,0,2:T(8,128)S(1)} %bitcast_select_fusion.14, f32[6,64,64]{2,1,0:T(8,128)S(1)} %copy-done.21), kind=kOutput, calls=%fused_computation.65 | convolution fusion | flops 301989888 | bytes 5799936 | tf_op jit(solution)/shard_map/vrz,rp->vpz/dot_general | solution.py:29
  58.4 5.8 %fusion.30 = f32[12,512,64]{1,2,0:T(8,128)} fusion(f32[12,64,512]{1,0,2:T(8,128)S(1)} %bitcast_select_fusion.15, f32[6,64,64]{2,1,0:T(8,128)S(1)} %copy-done.21), kind=kOutput, calls=%fused_computation.67 | convolution fusion | flops 301989888 | bytes 5799936 | tf_op jit(solution)/shard_map/vrz,rp->vpz/dot_general | solution.py:29
  64.2 5.5 %gather_fusion.1 = f32[512,12,64]{2,1,0:T(8,128)} fusion(f32[12,64,640]{1,0,2:T(8,128)} %copy.161, s32[1024]{0:T(1024)S(1)} %pad_clamp_fusion.4), kind=kCustom, calls=%fused_computation.1.clone | custom fusion | bytes 3147776 | tf_op jit(solution)/shard_map/jit(_take)/gather | solution.py:27
  74.9 5.8 %fusion.32 = f32[12,512,64]{1,2,0:T(8,128)} fusion(f32[12,64,512]{1,0,2:T(8,128)S(1)} %bitcast_select_fusion.16, f32[6,64,64]{2,1,0:T(8,128)S(1)} %copy-done.21), kind=kOutput, calls=%fused_computation.69 | convolution fusion | flops 301989888 | bytes 5799936 | tf_op jit(solution)/shard_map/vrz,rp->vpz/dot_general | solution.py:29
  80.7 5.5 %gather_fusion = f32[512,12,64]{2,1,0:T(8,128)} fusion(f32[12,64,640]{1,0,2:T(8,128)} %copy.161, s32[1024]{0:T(1024)S(1)} %pad_clamp_fusion.5), kind=kCustom, calls=%fused_computation.clone | custom fusion | bytes 3147776 | tf_op jit(solution)/shard_map/jit(_take)/gather | solution.py:27
  91.3 5.7 %fusion.34 = f32[12,512,64]{1,2,0:T(8,128)} fusion(f32[12,64,512]{1,0,2:T(8,128)S(1)} %bitcast_select_fusion.17, f32[6,64,64]{2,1,0:T(8,128)S(1)} %copy-done.21), kind=kOutput, calls=%fused_computation.71 | convolution fusion | flops 301989888 | bytes 5799936 | tf_op jit(solution)/shard_map/vrz,rp->vpz/dot_general | solution.py:29
  97.0 5.5 %gather_fusion.4 = f32[512,12,64]{2,1,0:T(8,128)} fusion(f32[12,64,640]{1,0,2:T(8,128)} %copy.161, s32[1024]{0:T(1024)S(1)} %pad_clamp_fusion.1), kind=kCustom, calls=%fused_computation.4.clone | custom fusion | bytes 3147776 | tf_op jit(solution)/shard_map/jit(_take)/gather | solution.py:27
  107.8 5.7 %fusion.26 = f32[12,512,64]{1,2,0:T(8,128)} fusion(f32[12,64,512]{1,0,2:T(8,128)S(1)} %bitcast_select_fusion.13, f32[6,64,64]{2,1,0:T(8,128)S(1)} %copy-done.21), kind=kOutput, calls=%fused_computation.63 | convolution fusion | flops 301989888 | bytes 5799936 | tf_op jit(solution)/shard_map/vrz,rp->vpz/dot_general | solution.py:29
  113.5 5.5 %gather_fusion.5 = f32[512,12,64]{2,1,0:T(8,128)} fusion(f32[12,64,640]{1,0,2:T(8,128)} %copy.161, s32[1024]{0:T(1024)S(1)} %pad_clamp_fusion), kind=kCustom, calls=%fused_computation.5.clone | custom fusion | bytes 3147776 | tf_op jit(solution)/shard_map/jit(_take)/gather | solution.py:27
  119.0 6.0 %bitcast_select_fusion.12 = f32[12,64,512]{1,0,2:T(8,128)S(1)} fusion(f32[512,12,64]{2,1,0:T(8,128)} %gather_fusion.5, pred[512]{0:T(512)(128)(4,1)S(1)} %get-tuple-element.12, pred[512]{0:T(512)(128)(4,1)S(1)} %get-tuple-element.6), kind=kLoop, calls=%fused_computation.31 | loop fusion | flops 786432 | bytes 3146752 | tf_op jit(solution)/shard_map/jit(_where)/select_n | solution.py:28
  139.9 9.6 %collective-permute-done.2 = f32[12,64,64]{2,1,0:T(8,128)S(1)} collective-permute-done((f32[12,64,64]{2,1,0:T(8,128)S(1)}, f32[12,64,64]{2,1,0:T(8,128)S(1)}, u32[]{:S(2)}, u32[]{:S(2)}) %collective-permute-start.2) | collective-permute-done | bytes 196640 | tf_op jit(solution)/shard_map/ppermute | solution.py:12
  154.5 6.1 %copy.180 = f32[12,64,640]{1,0,2:T(8,128)} copy(f32[12,64,640]{2,1,0:T(8,128)} %pad_maximum_fusion.1) | data formatting | bytes 3932160 | tf_op jit(solution)/shard_map/concatenate | solution.py:16
  160.7 5.6 %gather_fusion.9 = f32[512,12,64]{2,1,0:T(8,128)} fusion(f32[12,64,640]{1,0,2:T(8,128)} %copy.180, s32[1024]{0:T(1024)S(1)} %pad_clamp_fusion.2), kind=kCustom, calls=%fused_computation.9.clone | custom fusion | bytes 3147776 | tf_op jit(solution)/shard_map/jit(_take)/gather | solution.py:27
  171.6 5.5 %gather_fusion.7 = f32[512,12,64]{2,1,0:T(8,128)} fusion(f32[12,64,640]{1,0,2:T(8,128)} %copy.180, s32[1024]{0:T(1024)S(1)} %pad_clamp_fusion.4), kind=kCustom, calls=%fused_computation.7.clone | custom fusion | bytes 3147776 | tf_op jit(solution)/shard_map/jit(_take)/gather | solution.py:27
  177.1 5.5 %gather_fusion.6 = f32[512,12,64]{2,1,0:T(8,128)} fusion(f32[12,64,640]{1,0,2:T(8,128)} %copy.180, s32[1024]{0:T(1024)S(1)} %pad_clamp_fusion.5), kind=kCustom, calls=%fused_computation.6.clone | custom fusion | bytes 3147776 | tf_op jit(solution)/shard_map/jit(_take)/gather | solution.py:27
  182.6 5.5 %gather_fusion.10 = f32[512,12,64]{2,1,0:T(8,128)} fusion(f32[12,64,640]{1,0,2:T(8,128)} %copy.180, s32[1024]{0:T(1024)S(1)} %pad_clamp_fusion.1), kind=kCustom, calls=%fused_computation.10.clone | custom fusion | bytes 3147776 | tf_op jit(solution)/shard_map/jit(_take)/gather | solution.py:27
  188.0 5.6 %gather_fusion.11 = f32[512,12,64]{2,1,0:T(8,128)} fusion(f32[12,64,640]{1,0,2:T(8,128)} %copy.180, s32[1024]{0:T(1024)S(1)} %pad_clamp_fusion), kind=kCustom, calls=%fused_computation.11.clone | custom fusion | bytes 3147776 | tf_op jit(solution)/shard_map/jit(_take)/gather | solution.py:27
  249.8 9.6 %collective-permute-done.4 = f32[12,64,64]{2,1,0:T(8,128)S(1)} collective-permute-done((f32[12,64,64]{2,1,0:T(8,128)S(1)}, f32[12,64,64]{2,1,0:T(8,128)S(1)}, u32[]{:S(2)}, u32[]{:S(2)}) %collective-permute-start.4) | collective-permute-done | bytes 196640 | tf_op jit(solution)/shard_map/ppermute | solution.py:12
  264.5 6.1 %copy.193 = f32[12,64,640]{1,0,2:T(8,128)} copy(f32[12,64,640]{2,1,0:T(8,128)} %pad_maximum_fusion.2) | data formatting | bytes 3932160 | tf_op jit(solution)/shard_map/concatenate | solution.py:16
  270.7 5.6 %gather_fusion.12 = f32[512,12,64]{2,1,0:T(8,128)} fusion(f32[12,64,640]{1,0,2:T(8,128)} %copy.193, s32[1024]{0:T(1024)S(1)} %pad_clamp_fusion.5), kind=kCustom, calls=%fused_computation.12.clone | custom fusion | bytes 3147776 | tf_op jit(solution)/shard_map/jit(_take)/gather | solution.py:27
  276.2 5.5 %gather_fusion.13 = f32[512,12,64]{2,1,0:T(8,128)} fusion(f32[12,64,640]{1,0,2:T(8,128)} %copy.193, s32[1024]{0:T(1024)S(1)} %pad_clamp_fusion.4), kind=kCustom, calls=%fused_computation.13.clone | custom fusion | bytes 3147776 | tf_op jit(solution)/shard_map/jit(_take)/gather | solution.py:27
  281.7 5.5 %gather_fusion.14 = f32[512,12,64]{2,1,0:T(8,128)} fusion(f32[12,64,640]{1,0,2:T(8,128)} %copy.193, s32[1024]{0:T(1024)S(1)} %pad_clamp_fusion.3), kind=kCustom, calls=%fused_computation.14.clone | custom fusion | bytes 3147776 | tf_op jit(solution)/shard_map/jit(_take)/gather | solution.py:27
  292.6 5.6 %gather_fusion.16 = f32[512,12,64]{2,1,0:T(8,128)} fusion(f32[12,64,640]{1,0,2:T(8,128)} %copy.193, s32[1024]{0:T(1024)S(1)} %pad_clamp_fusion.1), kind=kCustom, calls=%fused_computation.16.clone | custom fusion | bytes 3147776 | tf_op jit(solution)/shard_map/jit(_take)/gather | solution.py:27
  298.1 5.5 %gather_fusion.17 = f32[512,12,64]{2,1,0:T(8,128)} fusion(f32[12,64,640]{1,0,2:T(8,128)} %copy.193, s32[1024]{0:T(1024)S(1)} %pad_clamp_fusion), kind=kCustom, calls=%fused_computation.17.clone | custom fusion | bytes 3147776 | tf_op jit(solution)/shard_map/jit(_take)/gather | solution.py:27
  303.6 7.0 %bitcast_select_fusion.4 = (f32[12,64,512]{1,0,2:T(8,128)S(1)}, f32[12,64,512]{1,0,2:T(8,128)S(1)}) fusion(f32[512,12,64]{2,1,0:T(8,128)} %gather_fusion.13, pred[512]{0:T(512)(128)(4,1)S(1)} %get-tuple-element.16, pred[512]{0:T(512)(128)(4,1)S(1)} %get-tuple-element.9, f32[512,12,64]{2,1,0:T(8,128)} %gather_fusion.12, ...), kind=kLoop, calls=%fused_computation.23 | loop fusion | flops 1572864 | bytes 6293504 | tf_op jit(solution)/shard_map/jit(_where)/select_n | solution.py:28
  340.7 6.3 %fusion.37 = f32[12,64,512]{2,1,0:T(8,128)} fusion(f32[12,64,512]{2,1,0:T(8,128)S(1)} %fusion.39, f32[12,512,64]{1,2,0:T(8,128)S(1)} %fusion.2, f32[12,512,64]{1,2,0:T(8,128)S(1)} %fusion.4, f32[12,512,64]{1,2,0:T(8,128)S(1)} %fusion.6, f32[12,512,64]{1,2,0:T(8,128)S(1)} %fusion.8, f32[12,512,64]{1,2,0:T(8,128)S(1)} %copy-done.14, ...), kind=kOutput, calls=%fused_computation.80 | convolution fusion | flops 305922048 | bytes 18382848 | tf_op jit(solution)/shard_map/vrz,rp->vpz/dot_general | solution.py:29
  360.6 20.0 %all-to-all-done = f32[4,1,98304]{2,1,0:T(1,128)S(1)} async-done(((f32[4,1,98304]{2,1,0:T(1,128)}), f32[4,1,98304]{2,1,0:T(1,128)S(1)}, u32[]{:S(2)}, u32[]{:S(2)}) %all-to-all-start) | async-done | bytes 1572896 | tf_op jit(solution)/shard_map/all_to_all | solution.py:57
  399.2 22.5 %all_to_all.36 = f32[48,64,128]{2,1,0:T(8,128)S(1)} all-to-all(f32[48,64,128]{2,1,0:T(8,128)S(1)} %scatter_fusion), channel_id=1, replica_groups=mesh['zone'=8,'var'=4] {'var'}, dimensions={0} | all-to-all | bytes 3145728 | tf_op jit(solution)/shard_map/all_to_all | solution.py:59
  (125 shorter events, 197.3 us)
Async XLA Ops:
  0.0 11.1 %copy-start = (f32[64,64]{1,0:T(8,128)S(1)}, f32[64,64]{1,0:T(8,128)}, u32[]{:S(2)}) copy-start(f32[64,64]{1,0:T(8,128)} %param.10) | copy-start | bytes 49156
  0.0 24.6 %copy-start.1 = (f32[12,64,512]{2,1,0:T(8,128)S(1)}, f32[12,64,512]{2,1,0:T(8,128)}, u32[]{:S(2)}) copy-start(f32[12,64,512]{2,1,0:T(8,128)} %param.8) | copy-start | bytes 4718596
  2.2 20.5 %collective-permute-start = (f32[12,64,64]{2,1,0:T(8,128)}, f32[12,64,64]{2,1,0:T(8,128)}, u32[]{:S(2)}, u32[]{:S(2)}) collective-permute-start(f32[12,64,64]{2,1,0:T(8,128)} %get-tuple-element.28), channel_id=1, source_target_pairs={{0,4},{4,8},{8,12},{12,16},{16,20},{20,24},{24,28},{1,5},{5,9},{9,... | collective-permute-start | bytes 589832 | tf_op jit(solution)/shard_map/ppermute | solution.py:12
  5.7 19.0 %collective-permute-start.1 = (f32[12,64,64]{2,1,0:T(8,128)}, f32[12,64,64]{2,1,0:T(8,128)}, u32[]{:S(2)}, u32[]{:S(2)}) collective-permute-start(f32[12,64,64]{2,1,0:T(8,128)} %get-tuple-element.29), channel_id=1, source_target_pairs={{4,0},{8,4},{12,8},{16,12},{20,16},{24,20},{28,24},{5,1},{9,5},{13... | collective-permute-start | bytes 589832 | tf_op jit(solution)/shard_map/ppermute | solution.py:15
  45.0 5.1 %copy-start.21 = (f32[6,64,64]{2,1,0:T(8,128)S(1)}, f32[6,64,64]{2,1,0:T(8,128)}, u32[]{:S(2)}) copy-start(f32[6,64,64]{2,1,0:T(8,128)} %param.11) | copy-start | bytes 294916
  50.1 5.8 %copy-start.13 = (f32[512,12,64]{2,1,0:T(8,128)S(1)}, f32[512,12,64]{2,1,0:T(8,128)}, u32[]{:S(2)}) copy-start(f32[512,12,64]{2,1,0:T(8,128)} %gather_fusion.2) | copy-start | bytes 4718596
  119.0 6.0 %copy-start.16 = (f32[12,512,64]{1,2,0:T(8,128)S(1)}, f32[12,512,64]{1,2,0:T(8,128)}, u32[]{:S(2)}) copy-start(f32[12,512,64]{1,2,0:T(8,128)} %fusion.28) | copy-start | bytes 4718596
  119.0 6.0 %copy-start.17 = (f32[12,512,64]{1,2,0:T(8,128)S(1)}, f32[12,512,64]{1,2,0:T(8,128)}, u32[]{:S(2)}) copy-start(f32[12,512,64]{1,2,0:T(8,128)} %fusion.30) | copy-start | bytes 4718596
  119.0 6.1 %copy-start.18 = (f32[12,512,64]{1,2,0:T(8,128)S(1)}, f32[12,512,64]{1,2,0:T(8,128)}, u32[]{:S(2)}) copy-start(f32[12,512,64]{1,2,0:T(8,128)} %fusion.32) | copy-start | bytes 4718596
  119.0 6.1 %copy-start.19 = (f32[12,512,64]{1,2,0:T(8,128)S(1)}, f32[12,512,64]{1,2,0:T(8,128)}, u32[]{:S(2)}) copy-start(f32[12,512,64]{1,2,0:T(8,128)} %fusion.34) | copy-start | bytes 4718596
  119.0 6.1 %copy-start.20 = (f32[12,512,64]{1,2,0:T(8,128)S(1)}, f32[12,512,64]{1,2,0:T(8,128)}, u32[]{:S(2)}) copy-start(f32[12,512,64]{1,2,0:T(8,128)} %fusion.26) | copy-start | bytes 4718596
  130.1 22.5 %copy-start.2 = (f32[12,64,512]{2,1,0:T(8,128)}, f32[12,64,512]{2,1,0:T(8,128)S(1)}, u32[]{:S(2)}) copy-start(f32[12,64,512]{2,1,0:T(8,128)S(1)} %fusion.40) | copy-start | bytes 4718596
  130.3 19.2 %collective-permute-start.2 = (f32[12,64,64]{2,1,0:T(8,128)S(1)}, f32[12,64,64]{2,1,0:T(8,128)S(1)}, u32[]{:S(2)}, u32[]{:S(2)}) collective-permute-start(f32[12,64,64]{2,1,0:T(8,128)S(1)} %get-tuple-element.26), channel_id=1, source_target_pairs={{0,4},{4,8},{8,12},{12,16},{16,20},{20,24},{24,28},{1,5},{5,9},{9,... | collective-permute-start | bytes 589832 | tf_op jit(solution)/shard_map/ppermute | solution.py:12
  132.9 19.7 %collective-permute-start.3 = (f32[12,64,64]{2,1,0:T(8,128)S(1)}, f32[12,64,64]{2,1,0:T(8,128)S(1)}, u32[]{:S(2)}, u32[]{:S(2)}) collective-permute-start(f32[12,64,64]{2,1,0:T(8,128)S(1)} %get-tuple-element.27), channel_id=1, source_target_pairs={{4,0},{8,4},{12,8},{16,12},{20,16},{24,20},{28,24},{5,1},{9,5},{13... | collective-permute-start | bytes 589832 | tf_op jit(solution)/shard_map/ppermute | solution.py:15
  198.7 4.7 %copy-start.12 = (f32[512,12,64]{2,1,0:T(8,128)S(1)}, f32[512,12,64]{2,1,0:T(8,128)}, u32[]{:S(2)}) copy-start(f32[512,12,64]{2,1,0:T(8,128)} %gather_fusion.8) | copy-start | bytes 4718596
  205.9 4.7 %copy-start.11 = (f32[512,12,64]{2,1,0:T(8,128)S(1)}, f32[512,12,64]{2,1,0:T(8,128)}, u32[]{:S(2)}) copy-start(f32[512,12,64]{2,1,0:T(8,128)} %gather_fusion.7) | copy-start | bytes 4718596
  213.2 4.7 %copy-start.10 = (f32[512,12,64]{2,1,0:T(8,128)S(1)}, f32[512,12,64]{2,1,0:T(8,128)}, u32[]{:S(2)}) copy-start(f32[512,12,64]{2,1,0:T(8,128)} %gather_fusion.6) | copy-start | bytes 4718596
  220.4 4.7 %copy-start.9 = (f32[512,12,64]{2,1,0:T(8,128)S(1)}, f32[512,12,64]{2,1,0:T(8,128)}, u32[]{:S(2)}) copy-start(f32[512,12,64]{2,1,0:T(8,128)} %gather_fusion.10) | copy-start | bytes 4718596
  227.8 4.7 %copy-start.8 = (f32[512,12,64]{2,1,0:T(8,128)S(1)}, f32[512,12,64]{2,1,0:T(8,128)}, u32[]{:S(2)}) copy-start(f32[512,12,64]{2,1,0:T(8,128)} %gather_fusion.11) | copy-start | bytes 4718596
  232.4 2.5 copy-start.3
  232.4 2.5 copy-start.15
  240.3 19.2 %collective-permute-start.4 = (f32[12,64,64]{2,1,0:T(8,128)S(1)}, f32[12,64,64]{2,1,0:T(8,128)S(1)}, u32[]{:S(2)}, u32[]{:S(2)}) collective-permute-start(f32[12,64,64]{2,1,0:T(8,128)S(1)} %get-tuple-element.24), channel_id=1, source_target_pairs={{0,4},{4,8},{8,12},{12,16},{16,20},{20,24},{24,28},{1,5},{5,9},{9,... | collective-permute-start | bytes 589832 | tf_op jit(solution)/shard_map/ppermute | solution.py:12
  242.2 20.3 %collective-permute-start.5 = (f32[12,64,64]{2,1,0:T(8,128)S(1)}, f32[12,64,64]{2,1,0:T(8,128)S(1)}, u32[]{:S(2)}, u32[]{:S(2)}) collective-permute-start(f32[12,64,64]{2,1,0:T(8,128)S(1)} %get-tuple-element.25), channel_id=1, source_target_pairs={{4,0},{8,4},{12,8},{16,12},{20,16},{24,20},{28,24},{5,1},{9,5},{13... | collective-permute-start | bytes 589832 | tf_op jit(solution)/shard_map/ppermute | solution.py:15
  310.6 9.3 %copy-start.6 = (f32[512,12,64]{2,1,0:T(8,128)S(1)}, f32[512,12,64]{2,1,0:T(8,128)}, u32[]{:S(2)}) copy-start(f32[512,12,64]{2,1,0:T(8,128)} %gather_fusion.14) | copy-start | bytes 4718596
  310.6 9.3 %copy-start.7 = (f32[512,12,64]{2,1,0:T(8,128)S(1)}, f32[512,12,64]{2,1,0:T(8,128)}, u32[]{:S(2)}) copy-start(f32[512,12,64]{2,1,0:T(8,128)} %gather_fusion.15) | copy-start | bytes 4718596
  323.3 9.3 %copy-start.4 = (f32[512,12,64]{2,1,0:T(8,128)S(1)}, f32[512,12,64]{2,1,0:T(8,128)}, u32[]{:S(2)}) copy-start(f32[512,12,64]{2,1,0:T(8,128)} %gather_fusion.16) | copy-start | bytes 4718596
  323.3 9.3 %copy-start.5 = (f32[512,12,64]{2,1,0:T(8,128)S(1)}, f32[512,12,64]{2,1,0:T(8,128)}, u32[]{:S(2)}) copy-start(f32[512,12,64]{2,1,0:T(8,128)} %gather_fusion.17) | copy-start | bytes 4718596
  336.1 4.6 %copy-start.14 = (f32[12,512,64]{1,2,0:T(8,128)S(1)}, f32[12,512,64]{1,2,0:T(8,128)}, u32[]{:S(2)}) copy-start(f32[12,512,64]{1,2,0:T(8,128)} %fusion.73) | copy-start | bytes 4718596
  356.8 23.9 %all-to-all-start = ((f32[4,1,98304]{2,1,0:T(1,128)}), f32[4,1,98304]{2,1,0:T(1,128)S(1)}, u32[]{:S(2)}, u32[]{:S(2)}) async-start(f32[4,1,98304]{2,1,0:T(1,128)} %reshape.318), calls=%async_computation | async-start | bytes 3145728 | tf_op jit(solution)/shard_map/all_to_all | solution.py:57
  389.9 3.4 copy-start.22
  389.9 5.2 %copy-start.23 = (f32[12,48]{1,0:T(8,128)S(1)}, f32[12,48]{1,0:T(8,128)}, u32[]{:S(2)}) copy-start(f32[12,48]{1,0:T(8,128)} %param.13) | copy-start | bytes 6916
where the time goes:
time: 428 us; the launch traced here: 423 us
  local copies, waits for them, and re-layouts  140 us (33%)
  matrix products  104 us (24%)
  other arithmetic  76.1 us (18%)
  waiting for transfers between devices  56.1 us (13%)
  starting transfers between devices  24 us (6%)
  blocking collectives  22.5 us (5%)
    gather x18, local copies, waits for them, and re-layouts, advect_operator(): neighbour = jnp.take(extended, local_index, axis=2)  98.8 us
    dot_general x18, matrix products, advect_operator(): jnp.einsum('vrz,rp->vpz', neighbour, face_lift[face], precision=lax.Preci...  91.7 us
    select_n x15, other arithmetic, advect_operator(): jnp.where(face_index[None, None, :] >= 0, neighbour, jnp.float32(0.0))  61 us
    ppermute x3, waiting for transfers between devices, padded(): lax.ppermute(lax.slice_in_dim(block, block.shape[dim] - width, None, axis...  28 us
    all_to_all x1, blocking collectives, per_device(): lax.all_to_all(renewed, 'var', split_axis=0, concat_axis=2, tiled=True)  22.5 us
    all_to_all x1, waiting for transfers between devices, per_device(): lax.all_to_all(advected, 'var', split_axis=2, concat_axis=0, tiled=True)  20 us
    concatenate x3, local copies, waits for them, and re-layouts, padded(): block = jnp.concatenate([low, block, high], axis=dim)  18.5 us
    ppermute x3, starting transfers between devices, padded(): lax.ppermute(lax.slice_in_dim(block, 0, width, axis=dim), axis, backward)  12.3 us
  transfers between devices with their start and end apart: 7, of which 7 were waited for; matrix products, arithmetic and copies ran while one was open for 2% of the time, Pallas kernels for 0%

commit v1 on v0

v1 whole, which is shorter than its diff:
```python
import functools

import jax
import jax.numpy as jnp
from jax import lax
from jax.experimental import pallas as pl
from jax.experimental.pallas import tpu as pltpu
from jax.sharding import PartitionSpec as P

F32 = jnp.float32
BF16 = jnp.bfloat16
MESH = pl.DeviceIdType.MESH
ROT = 4
TILE = 16


def split(x):
    hi = x.astype(BF16)
    return hi, (x - hi.astype(F32)).astype(BF16)


def kernel(sizes, adj_ref, op_ref, schmid_ref, hard_ref, h_ref, out_ref, cur, acc, lcat, wown, wmer,
           ohown, ohmer, hsend, hrecv, msg, mrecv, buf, tb,
           hs_sem, hr_sem, m_sem, mr_sem, x_sem, xr_sem, t_sem, tr_sem):
    zones_n, chips_n, vl, pts, local, faces, slips = sizes
    rim = local // 8
    lane = 2 * rim
    blk = 2 * lane
    half = vl * pts // 2
    zone = lax.axis_index("zone")
    var = lax.axis_index("var")
    chip = var // 2
    core = var % 2
    mate = chip * 2 + (1 - core)
    has_left = zone > 0
    has_right = zone < zones_n - 1
    low = lax.broadcasted_iota(jnp.int32, (pts, lane), 1) < rim

    barrier = pltpu.get_barrier_semaphore()

    @pl.when(has_left)
    def _():
        pl.semaphore_signal(barrier, inc=1, device_id={"zone": zone - 1}, device_id_type=MESH)

    @pl.when(has_right)
    def _():
        pl.semaphore_signal(barrier, inc=1, device_id={"zone": zone + 1}, device_id_type=MESH)

    pl.semaphore_signal(barrier, inc=1, device_id={"var": mate}, device_id_type=MESH)
    for d in range(1, chips_n):
        peer = ((chip + d) % chips_n) * 2 + core
        pl.semaphore_signal(barrier, inc=1, device_id={"var": peer}, device_id_type=MESH)

    def halo_copy(s, side):
        target = zone + 1 if side == 0 else zone - 1
        return pltpu.make_async_remote_copy(
            src_ref=hsend.at[s, side], dst_ref=hrecv.at[s, side],
            send_sem=hs_sem.at[s, side], recv_sem=hr_sem.at[s, side],
            device_id={"zone": target}, device_id_type=MESH)

    def pack_edges(s, src):
        def body(i, _):
            top = pl.ds(pl.multiple_of(i * pts, pts), pts)
            bot = pl.ds(pl.multiple_of(half + i * pts, pts), pts)
            hsend[s, 0, top, :] = jnp.where(
                low, pltpu.roll(src[top, local - lane:local], rim, 1), src[bot, local - lane:local])
            hsend[s, 1, top, :] = jnp.where(
                low, src[top, 0:lane], pltpu.roll(src[bot, 0:lane], rim, 1))
            return 0
        lax.fori_loop(0, vl // 2, body, 0)

    def start_halo(s):
        @pl.when(has_right)
        def _():
            halo_copy(s, 0).start()

        @pl.when(has_left)
        def _():
            halo_copy(s, 1).start()

    def wait_halo(s):
        @pl.when(has_left)
        def _():
            halo_copy(s, 0).wait_recv()

        @pl.when(has_right)
        def _():
            halo_copy(s, 1).wait_recv()

    pack_edges(0, h_ref)

    @pl.when(jnp.logical_not(has_left))
    def _():
        for s in range(3):
            hrecv[s, 0] = jnp.zeros((half, lane), F32)

    @pl.when(jnp.logical_not(has_right))
    def _():
        for s in range(3):
            hrecv[s, 1] = jnp.zeros((half, lane), F32)

    pl.semaphore_wait(barrier, chips_n + has_left.astype(jnp.int32) + has_right.astype(jnp.int32))
    start_halo(0)

    rows_all = (faces + 1) * pts
    op_hi, op_lo = split(op_ref[...])
    first = lax.broadcasted_iota(jnp.int32, (rows_all, 4 * pts), 1) < 2 * pts
    lcat[...] = jnp.where(first, op_hi.astype(F32), op_lo.astype(F32)).astype(BF16)

    offset = zone * local
    k_own = lax.broadcasted_iota(jnp.int32, (blk, blk), 0)
    k_mer = lax.broadcasted_iota(jnp.int32, (lane, blk), 0)
    for b in range(2):
        src_mer = jnp.where(k_mer < rim, blk * (b + 1) + k_mer, blk * b - lane + k_mer)
        for f in range(faces):
            adj = adj_ref[f:f + 1, b * blk:(b + 1) * blk]
            adj = jnp.where(adj >= 0, adj - offset, -4 * local)
            ohown[b, f * blk:(f + 1) * blk, :] = jnp.where(
                k_own + b * blk == adj, 1.0, 0.0).astype(BF16)
            ohmer[b, f * lane:(f + 1) * lane, :] = jnp.where(
                src_mer == adj, 1.0, 0.0).astype(BF16)

    def v_rows(v):
        return pl.ds(pl.multiple_of(v * pts, pts), pts)

    def put(ref, v, col, width, w):
        hi, lo = split(w)
        ref[pl.ds(pl.multiple_of(v * 2 * pts, pts), pts), col:col + width] = hi
        ref[pl.ds(pl.multiple_of(v * 2 * pts + pts, pts), pts), col:col + width] = lo

    def lift_own(src):
        def body(v, _):
            rows = v_rows(v)
            for b in range(2):
                u = src[rows, b * blk:(b + 1) * blk]
                hi, lo = split(u)
                w = jnp.dot(lcat[...], jnp.concatenate([hi, lo, hi, lo], axis=0),
                            preferred_element_type=F32)
                acc[rows, b * blk:(b + 1) * blk] = u + w[faces * pts:]
                for f in range(faces):
                    put(wown, v, (b * faces + f) * blk, blk, w[f * pts:(f + 1) * pts])
            return 0
        lax.fori_loop(0, vl, body, 0)

    def lift_merged(s, src):
        def one(v, left, right):
            rows = v_rows(v)
            m0 = jnp.where(low, src[rows, blk:blk + lane], left)
            m1 = jnp.where(low, right, src[rows, blk - lane:blk])
            hi, lo = split(jnp.concatenate([m0, m1], axis=1))
            w = jnp.dot(lcat[0:faces * pts, :], jnp.concatenate([hi, lo, hi, lo], axis=0),
                        preferred_element_type=F32)
            for b in range(2):
                for f in range(faces):
                    put(wmer, v, (b * faces + f) * lane, lane,
                        w[f * pts:(f + 1) * pts, b * lane:(b + 1) * lane])

        def body(i, _):
            rows = v_rows(i)
            left, right = hrecv[s, 0, rows, :], hrecv[s, 1, rows, :]
            one(i, pltpu.roll(left, rim, 1), right)
            one(i + vl // 2, left, pltpu.roll(right, rim, 1))
            return 0
        lax.fori_loop(0, vl // 2, body, 0)

    group = 4 if vl % 4 == 0 else 3 if vl % 3 == 0 else 1

    def select(lhs, rhs, b, width, finish):
        def body(g, _):
            r = jnp.dot(
                lhs[pl.ds(pl.multiple_of(g * group * 2 * pts, 2 * pts), group * 2 * pts),
                    b * faces * width:(b + 1) * faces * width],
                rhs[b], preferred_element_type=F32)
            for j in range(group):
                part = r[2 * j * pts:(2 * j + 1) * pts] + r[(2 * j + 1) * pts:(2 * j + 2) * pts]
                finish(v_rows(g * group + j), slice(b * blk, (b + 1) * blk), part)
            return 0
        lax.fori_loop(0, vl // group, body, 0)

    def add(rows, cols, part):
        acc[rows, cols] += part

    def finish_for(s):
        def finish(rows, cols, part):
            total = acc[rows, cols] + part
            if s == 0:
                cur[rows, cols] = total
            elif s == 1:
                cur[rows, cols] = 0.75 * h_ref[rows, cols] + 0.25 * total
            else:
                cur[rows, cols] = h_ref[rows, cols] * (1.0 / 3.0) + (2.0 / 3.0) * total
        return finish

    def shear_chunk(col, dest, rot_row):
        def body(t, _):
            tr = pl.ds(pl.multiple_of(t * TILE, TILE), TILE)
            xs = [cur[pl.ds(pl.multiple_of(v * pts + t * TILE, TILE), TILE), pl.ds(col, lane)]
                  for v in range(vl)]
            for a in range(slips):
                y = xs[0] * schmid_ref[var * vl, a]
                for v in range(1, vl):
                    y = y + xs[v] * schmid_ref[var * vl + v, a]
                dest[a, tr, :] = y
            dest[rot_row, tr, :] = xs[0]
            return 0
        lax.fori_loop(0, pts // TILE, body, 0)

    def chunk_col(b, c):
        return pl.multiple_of(b * blk + c * lane, lane)

    def mate_copy(b):
        return pltpu.make_async_remote_copy(
            src_ref=msg.at[b], dst_ref=mrecv.at[b], send_sem=m_sem.at[b], recv_sem=mr_sem.at[b],
            device_id={"var": mate}, device_id_type=MESH)

    def chip_copy(b, d, slot):
        peer = ((chip + d) % chips_n) * 2 + core
        return pltpu.make_async_remote_copy(
            src_ref=buf.at[b, slot], dst_ref=buf.at[b, slot],
            send_sem=x_sem.at[b, d - 1], recv_sem=xr_sem.at[b, slot],
            device_id={"var": peer}, device_id_type=MESH)

    def tanh_copy(b, slot):
        return pltpu.make_async_remote_copy(
            src_ref=tb.at[b, slot], dst_ref=tb.at[b, slot],
            send_sem=t_sem.at[b], recv_sem=tr_sem.at[b],
            device_id={"var": mate}, device_id_type=MESH)

    def send_partial(b):
        shear_chunk(chunk_col(b, 1 - core), msg.at[b], slips)
        mate_copy(b).start()
        shear_chunk(chunk_col(b, core), buf.at[b, chip], slips + core)

    def send_chip(b):
        mate_copy(b).wait_recv()
        mine = buf.at[b, chip]
        for a in range(slips):
            mine[a] = mine[a] + mrecv[b, a]
        mine[slips + 1 - core] = mrecv[b, slips]
        for d in range(1, chips_n):
            chip_copy(b, d, chip).start()

    def renew(b):
        for d in range(1, chips_n):
            chip_copy(b, d, (chip + d) % chips_n).wait_recv()

        def body(t, _):
            tr = pl.ds(pl.multiple_of(t * TILE, TILE), TILE)
            ts = []
            for a in range(slips):
                y = buf[b, 0, a, tr, :]
                for c in range(1, chips_n):
                    y = y + buf[b, c, a, tr, :]
                ts.append(jnp.tanh(y))
                tb[b, core, a, tr, :] = ts[-1]
            total = None
            for k in range(ROT):
                y = buf[b, k // 2, slips + k % 2, tr, :]
                for a in range(slips):
                    y = y + ts[a] * hard_ref[a, k * vl]
                total = y * y if total is None else total + y * y
            tb[b, core, slips, tr, :] = 1.0 / jnp.maximum(jnp.sqrt(total), 1.0)
            return 0
        lax.fori_loop(0, pts // TILE, body, 0)
        tanh_copy(b, core).start()

    rotates = (jnp.full((TILE, lane), var, jnp.int32) < ROT)

    def write(b, c):
        col = chunk_col(b, c)

        def body(t, _):
            tr = pl.ds(pl.multiple_of(t * TILE, TILE), TILE)
            ts = [tb[b, c, a, tr, :] for a in range(slips)]
            for v in range(vl):
                rows = pl.ds(pl.multiple_of(v * pts + t * TILE, TILE), TILE)
                y = cur[rows, pl.ds(col, lane)]
                for a in range(slips):
                    y = y + ts[a] * hard_ref[a, var * vl + v]
                if v == 0:
                    y = jnp.where(rotates, y * tb[b, c, slips, tr, :], y)
                out_ref[rows, pl.ds(col, lane)] = y
            return 0
        lax.fori_loop(0, pts // TILE, body, 0)

    for s in range(3):
        src = h_ref if s == 0 else cur
        lift_own(src)
        for b in range(2):
            select(wown, ohown, b, blk, add)
        wait_halo(s)
        lift_merged(s, src)
        for b in range(2):
            select(wmer, ohmer, b, lane, finish_for(s))
            if s == 2:
                send_partial(b)
        if s < 2:
            pack_edges(s + 1, cur)
            start_halo(s + 1)

    for b in range(2):
        send_chip(b)
    for b in range(2):
        renew(b)
    for b in range(2):
        write(b, core)
    for b in range(2):
        tanh_copy(b, 1 - core).wait_recv()
        write(b, 1 - core)

    for s in range(3):
        @pl.when(has_right)
        def _():
            halo_copy(s, 0).wait_send()

        @pl.when(has_left)
        def _():
            halo_copy(s, 1).wait_send()
    for b in range(2):
        mate_copy(b).wait_send()
        tanh_copy(b, core).wait_send()
        for d in range(1, chips_n):
            chip_copy(b, d, chip).wait_send()


def per_device(zones_n, chips_n, history, adjacency, volume_op, face_lift, schmid_map, hardening):
    vl, pts, local = history.shape
    faces = face_lift.shape[0]
    slips = schmid_map.shape[1]
    lane, blk, half = local // 4, local // 2, vl * pts // 2
    ops = jnp.concatenate([face_lift, volume_op[None]], axis=0)
    ops = jnp.tile(jnp.swapaxes(ops, 1, 2).reshape((faces + 1) * pts, pts), (1, 4))
    vmem = pl.BlockSpec(memory_space=pltpu.VMEM)
    smem = pl.BlockSpec(memory_space=pltpu.SMEM)
    dma = pltpu.SemaphoreType.DMA
    out = pl.pallas_call(
        functools.partial(kernel, (zones_n, chips_n, vl, pts, local, faces, slips)),
        out_shape=jax.ShapeDtypeStruct((vl * pts, local), F32),
        in_specs=[vmem, vmem, smem, smem, vmem],
        out_specs=vmem,
        scratch_shapes=[
            pltpu.VMEM((vl * pts, local), F32),
            pltpu.VMEM((vl * pts, local), F32),
            pltpu.VMEM(((faces + 1) * pts, 4 * pts), BF16),
            pltpu.VMEM((vl * 2 * pts, 2 * faces * blk), BF16),
            pltpu.VMEM((vl * 2 * pts, 2 * faces * lane), BF16),
            pltpu.VMEM((2, faces * blk, blk), BF16),
            pltpu.VMEM((2, faces * lane, blk), BF16),
            pltpu.VMEM((3, 2, half, lane), F32),
            pltpu.VMEM((3, 2, half, lane), F32),
            pltpu.VMEM((2, slips + 1, pts, lane), F32),
            pltpu.VMEM((2, slips + 1, pts, lane), F32),
            pltpu.VMEM((2, chips_n, slips + 2, pts, lane), F32),
            pltpu.VMEM((2, 2, slips + 1, pts, lane), F32),
            dma((3, 2)), dma((3, 2)), dma((2,)), dma((2,)),
            dma((2, max(chips_n - 1, 1))), dma((2, chips_n)), dma((2,)), dma((2,)),
        ],
        compiler_params=pltpu.CompilerParams(
            collective_id=0, has_side_effects=True, vmem_limit_bytes=56 * 1024 * 1024),
    )(adjacency, ops, schmid_map, hardening, history.reshape(vl * pts, local))
    return out.reshape(vl, pts, local)


def solution(mesh):
    in_specs = (P("var", None, "zone"), P(None, "zone"), P(), P(), P(), P())
    out_specs = P("var", None, "zone")
    return jax.shard_map(
        functools.partial(per_device, mesh.shape["zone"], mesh.shape["var"] // 2),
        mesh=mesh, in_specs=in_specs, out_specs=out_specs, check_vma=False
    )
```

time: 428 us -> 84.2 us (0.20); the launches traced: 423 us -> 84 us
  local copies, waits for them, and re-layouts: 140 us -> 5.3 us
  matrix products: 104 us -> 0 us
  Pallas kernels: 0 us -> 77.7 us
  other arithmetic: 76.1 us -> 0.96 us
  waiting for transfers between devices: 56.1 us -> 0 us
  starting transfers between devices: 24 us -> 0 us
  blocking collectives: 22.5 us -> 0 us
    dot_general x23 -> x0, matrix products: 104 us -> none  [the longest x18 91.7 us: advect_operator(): jnp.einsum('vrz,rp->vpz', neighbour, face_lift[face], precision=lax.Preci...]
    gather x18 -> x0, local copies, waits for them, and re-layouts: 98.8 us -> none  [advect_operator(): neighbour = jnp.take(extended, local_index, axis=2)]
    pallas_call x0 -> x1, Pallas kernels: none -> 77.7 us  [per_device(): pl.pallas_call(functools.partial(kernel, (zones_n, chips_n, vl, pts, loca...]
    select_n x15 -> x0, other arithmetic: 61 us -> none  [advect_operator(): jnp.where(face_index[None, None, :] >= 0, neighbour, jnp.float32(0.0))]
    ppermute x6 -> x0, waiting for transfers between devices: 36 us -> none  [the longest x3 28 us: padded(): lax.ppermute(lax.slice_in_dim(block, block.shape[dim] - width, None, axis...]
    all_to_all x1 -> x0, blocking collectives: 22.5 us -> none  [per_device(): lax.all_to_all(renewed, 'var', split_axis=0, concat_axis=2, tiled=True)]
    ppermute x6 -> x0, starting transfers between devices: 20.2 us -> none  [the longest x3 12.3 us: padded(): lax.ppermute(lax.slice_in_dim(block, 0, width, axis=dim), axis, backward)]
    all_to_all x1 -> x0, waiting for transfers between devices: 20 us -> none  [per_device(): lax.all_to_all(advected, 'var', split_axis=2, concat_axis=0, tiled=True)]
  transfers between devices with their start and end apart: 7 -> 0, of which waited for: 7 -> 0; matrix products, arithmetic and copies ran while one was open for 2% -> 0% of each run, Pallas kernels for 0% -> 0%
where the time goes in v1:
time: 84.2 us; the launch traced here: 84 us
  Pallas kernels  77.7 us (92%)
  local copies, waits for them, and re-layouts  5.3 us (6%)
  other arithmetic  0.96 us (1%)
    pallas_call x1, Pallas kernels, per_device(): pl.pallas_call(functools.partial(kernel, (zones_n, chips_n, vl, pts, loca...  77.7 us
    unnamed x2, local copies, waits for them, and re-layouts  4.05 us

profile of v1, /device:TPU:16, one launch (start us, length us, event | category | flops | bytes accessed | tf_op | source)
XLA Modules:
  0.0 84.0 jit_solution(1486629099145523336)
XLA Ops:
  0.0 1.4 %copy.10.schmid_ref = f32[48,12]{1,0:T(8,128)} copy(f32[48,12]{0,1:T(8,128)} %param.10) | data formatting | bytes 4608 | tf_op args[4]
  1.4 1.0 %maximum_bitcast_fusion = f32[7,64,64]{1,2,0:T(8,128)S(1)} fusion(f32[1,64,64]{2,1,0:T(8,128)} %bitcast.11, f32[6,64,64]{2,1,0:T(8,128)} %param.9), kind=kLoop, calls=%fused_computation | loop fusion | flops 28672 | bytes 229376 | tf_op jit(solution)/shard_map/transpose | solution.py:332
  2.3 0.1 copy.8
  2.5 0.1 tile.10
  2.7 1.0 %copy.9.op_ref = f32[448,256]{1,0:T(8,128)} copy(f32[448,256]{0,1:T(8,128)S(1)} %bitcast.9) | data formatting | bytes 917504 | tf_op jit(solution)/shard_map/tile | solution.py:332
  3.6 77.7 %shard_map.64 = f32[768,512]{1,0:T(8,128)} custom-call(s32[6,512]{1,0:T(8,128)} %adj_ref.1, f32[448,256]{1,0:T(8,128)} %copy.9.op_ref, f32[48,12]{1,0:T(8,128)} %copy.10.schmid_ref, f32[12,48]{1,0:T(8,128)} %hard_ref.1, f32[768,512]{1,0:T(8,128)} %bitcast.10), custom_call_target="tpu_custom_call" | custom-call | tf_op jit(solution)/shard_map/pallas_call | solution.py:336
  81.3 2.7 %copy.12 = f32[12,64,512]{2,1,0:T(8,128)} copy(f32[12,64,512]{2,1,0:T(8,128)} %bitcast.8) | data formatting | bytes 3145728
  (1 shorter events, 0.0 us)

commit v2 on v1

--- a/solution.py
+++ b/solution.py
@@ -19,13 +19,11 @@
     return hi, (x - hi.astype(F32)).astype(BF16)
 
 
-def kernel(sizes, adj_ref, op_ref, schmid_ref, hard_ref, h_ref, out_ref, cur, acc, lcat, wown, wmer,
-           ohown, ohmer, hsend, hrecv, msg, mrecv, buf, tb,
+def kernel(sizes, adj_ref, op_ref, schmid_ref, hard_ref, h_ref, out_ref, one, two, cur, lcat, oh, hsend, hrecv, msg, mrecv, buf, tb,
            hs_sem, hr_sem, m_sem, mr_sem, x_sem, xr_sem, t_sem, tr_sem):
     zones_n, chips_n, vl, pts, local, faces, slips = sizes
     rim = local // 8
     lane = 2 * rim
-    blk = 2 * lane
     half = vl * pts // 2
     zone = lax.axis_index("zone")
     var = lax.axis_index("var")
@@ -102,94 +100,70 @@
     pl.semaphore_wait(barrier, chips_n + has_left.astype(jnp.int32) + has_right.astype(jnp.int32))
     start_halo(0)
 
-    rows_all = (faces + 1) * pts
     op_hi, op_lo = split(op_ref[...])
-    first = lax.broadcasted_iota(jnp.int32, (rows_all, 4 * pts), 1) < 2 * pts
-    lcat[...] = jnp.where(first, op_hi.astype(F32), op_lo.astype(F32)).astype(BF16)
+    upper = lax.broadcasted_iota(jnp.int32, op_ref.shape, 0) < pts
+    lcat[...] = jnp.where(upper, op_hi.astype(F32), op_lo.astype(F32)).astype(BF16)
 
     offset = zone * local
-    k_own = lax.broadcasted_iota(jnp.int32, (blk, blk), 0)
-    k_mer = lax.broadcasted_iota(jnp.int32, (lane, blk), 0)
-    for b in range(2):
-        src_mer = jnp.where(k_mer < rim, blk * (b + 1) + k_mer, blk * b - lane + k_mer)
+    k = lax.broadcasted_iota(jnp.int32, (2 * lane, lane), 0)
+    for b in range(4):
+        source = jnp.where(k < lane, lane * b + k,
+                           jnp.where(k < lane + rim, lane * b + k, lane * (b - 2) + k))
         for f in range(faces):
-            adj = adj_ref[f:f + 1, b * blk:(b + 1) * blk]
+            adj = adj_ref[f:f + 1, b * lane:(b + 1) * lane]
             adj = jnp.where(adj >= 0, adj - offset, -4 * local)
-            ohown[b, f * blk:(f + 1) * blk, :] = jnp.where(
-                k_own + b * blk == adj, 1.0, 0.0).astype(BF16)
-            ohmer[b, f * lane:(f + 1) * lane, :] = jnp.where(
-                src_mer == adj, 1.0, 0.0).astype(BF16)
+            oh[b, :, f * lane:(f + 1) * lane] = jnp.where(source == adj, 1.0, 0.0).astype(BF16)
 
     def v_rows(v):
         return pl.ds(pl.multiple_of(v * pts, pts), pts)
 
-    def put(ref, v, col, width, w):
-        hi, lo = split(w)
-        ref[pl.ds(pl.multiple_of(v * 2 * pts, pts), pts), col:col + width] = hi
-        ref[pl.ds(pl.multiple_of(v * 2 * pts + pts, pts), pts), col:col + width] = lo
-
-    def lift_own(src):
-        def body(v, _):
-            rows = v_rows(v)
-            for b in range(2):
-                u = src[rows, b * blk:(b + 1) * blk]
-                hi, lo = split(u)
-                w = jnp.dot(lcat[...], jnp.concatenate([hi, lo, hi, lo], axis=0),
-                            preferred_element_type=F32)
-                acc[rows, b * blk:(b + 1) * blk] = u + w[faces * pts:]
-                for f in range(faces):
-                    put(wown, v, (b * faces + f) * blk, blk, w[f * pts:(f + 1) * pts])
-            return 0
-        lax.fori_loop(0, vl, body, 0)
-
-    def lift_merged(s, src):
-        def one(v, left, right):
-            rows = v_rows(v)
-            m0 = jnp.where(low, src[rows, blk:blk + lane], left)
-            m1 = jnp.where(low, right, src[rows, blk - lane:blk])
-            hi, lo = split(jnp.concatenate([m0, m1], axis=1))
-            w = jnp.dot(lcat[0:faces * pts, :], jnp.concatenate([hi, lo, hi, lo], axis=0),
-                        preferred_element_type=F32)
-            for b in range(2):
-                for f in range(faces):
-                    put(wmer, v, (b * faces + f) * lane, lane,
-                        w[f * pts:(f + 1) * pts, b * lane:(b + 1) * lane])
+    def block(s, b, src, dst, halo=True):
+        cols = slice(b * lane, (b + 1) * lane)
 
         def body(i, _):
-            rows = v_rows(i)
-            left, right = hrecv[s, 0, rows, :], hrecv[s, 1, rows, :]
-            one(i, pltpu.roll(left, rim, 1), right)
-            one(i + vl // 2, left, pltpu.roll(right, rim, 1))
-            return 0
-        lax.fori_loop(0, vl // 2, body, 0)
-
-    group = 4 if vl % 4 == 0 else 3 if vl % 3 == 0 else 1
-
-    def select(lhs, rhs, b, width, finish):
-        def body(g, _):
-            r = jnp.dot(
-                lhs[pl.ds(pl.multiple_of(g * group * 2 * pts, 2 * pts), group * 2 * pts),
-                    b * faces * width:(b + 1) * faces * width],
-                rhs[b], preferred_element_type=F32)
-            for j in range(group):
-                part = r[2 * j * pts:(2 * j + 1) * pts] + r[(2 * j + 1) * pts:(2 * j + 2) * pts]
-                finish(v_rows(g * group + j), slice(b * blk, (b + 1) * blk), part)
-            return 0
-        lax.fori_loop(0, vl // group, body, 0)
-
-    def add(rows, cols, part):
-        acc[rows, cols] += part
-
-    def finish_for(s):
-        def finish(rows, cols, part):
-            total = acc[rows, cols] + part
-            if s == 0:
-                cur[rows, cols] = total
-            elif s == 1:
-                cur[rows, cols] = 0.75 * h_ref[rows, cols] + 0.25 * total
-            else:
-                cur[rows, cols] = h_ref[rows, cols] * (1.0 / 3.0) + (2.0 / 3.0) * total
-        return finish
+            owns, terms = [], []
+            for part in range(2):
+                rows = v_rows(i + part * (vl // 2))
+                own = src[rows, cols]
+                if b > 0:
+                    up = src[rows, (b - 1) * lane:b * lane]
+                elif halo:
+                    up = hrecv[s, 0, v_rows(i), :]
+                    up = pltpu.roll(up, rim, 1) if part == 0 else up
+                else:
+                    up = jnp.zeros((pts, lane), F32)
+                if b < 3:
+                    down = src[rows, (b + 1) * lane:(b + 2) * lane]
+                elif halo:
+                    down = hrecv[s, 1, v_rows(i), :]
+                    down = pltpu.roll(down, rim, 1) if part == 1 else down
+                else:
+                    down = jnp.zeros((pts, lane), F32)
+                owns.append(own)
+                terms.extend(split(jnp.concatenate([own, jnp.where(low, down, up)], axis=1)))
+            g = jnp.dot(jnp.concatenate(terms, axis=0), oh[b],
+                        preferred_element_type=F32).astype(BF16)
+            rhs = []
+            for part in range(2):
+                pieces = []
+                for t in range(2):
+                    q = 2 * part + t
+                    pieces += [g[q * pts:(q + 1) * pts, f * lane:(f + 1) * lane]
+                               for f in range(faces)]
+                    pieces.append(terms[q][:, 0:lane])
+                rhs.append(jnp.concatenate(pieces, axis=0))
+            r = jnp.dot(lcat[...], jnp.concatenate(rhs, axis=1), preferred_element_type=F32)
+            r = r[0:pts] + r[pts:2 * pts]
+            for part in range(2):
+                rows = v_rows(i + part * (vl // 2))
+                total = owns[part] + r[:, part * lane:(part + 1) * lane]
+                if s == 1:
+                    total = 0.75 * h_ref[rows, cols] + 0.25 * total
+                elif s == 2:
+                    total = h_ref[rows, cols] * (1.0 / 3.0) + (2.0 / 3.0) * total
+                dst[rows, cols] = total
+            return 0
+        lax.fori_loop(0, vl // 2, body, 0, unroll=3 if vl % 6 == 0 else 1)
 
     def shear_chunk(col, dest, rot_row):
         def body(t, _):
@@ -206,7 +180,7 @@
         lax.fori_loop(0, pts // TILE, body, 0)
 
     def chunk_col(b, c):
-        return pl.multiple_of(b * blk + c * lane, lane)
+        return pl.multiple_of((1 + c) * lane if b == 0 else 3 * c * lane, lane)
 
     def mate_copy(b):
         return pltpu.make_async_remote_copy(
@@ -283,28 +257,31 @@
             return 0
         lax.fori_loop(0, pts // TILE, body, 0)
 
-    for s in range(3):
-        src = h_ref if s == 0 else cur
-        lift_own(src)
-        for b in range(2):
-            select(wown, ohown, b, blk, add)
-        wait_halo(s)
-        lift_merged(s, src)
-        for b in range(2):
-            select(wmer, ohmer, b, lane, finish_for(s))
-            if s == 2:
-                send_partial(b)
-        if s < 2:
-            pack_edges(s + 1, cur)
-            start_halo(s + 1)
-
-    for b in range(2):
-        send_chip(b)
+    def both(s, blocks, src, dst, halo=True):
+        for b in blocks:
+            block(s, b, src, dst, halo)
+
+    both(0, (1, 2), h_ref, one)
+    wait_halo(0)
+    both(0, (0, 3), h_ref, one)
+    pack_edges(1, one)
+    start_halo(1)
+    both(1, (1, 2), one, two)
+    both(1, (0, 3), one, two, halo=False)
+    both(2, (1, 2), two, cur)
+    send_partial(0)
+    send_chip(0)
+    wait_halo(1)
+    both(1, (0, 3), one, two)
+    pack_edges(2, two)
+    start_halo(2)
+    wait_halo(2)
+    both(2, (0, 3), two, cur)
+    send_partial(1)
+    send_chip(1)
     for b in range(2):
         renew(b)
-    for b in range(2):
         write(b, core)
-    for b in range(2):
         tanh_copy(b, 1 - core).wait_recv()
         write(b, 1 - core)
 
@@ -327,9 +304,9 @@
     vl, pts, local = history.shape
     faces = face_lift.shape[0]
     slips = schmid_map.shape[1]
-    lane, blk, half = local // 4, local // 2, vl * pts // 2
+    lane, half = local // 4, vl * pts // 2
     ops = jnp.concatenate([face_lift, volume_op[None]], axis=0)
-    ops = jnp.tile(jnp.swapaxes(ops, 1, 2).reshape((faces + 1) * pts, pts), (1, 4))
+    ops = jnp.tile(ops.reshape((faces + 1) * pts, pts).T, (2, 2))
     vmem = pl.BlockSpec(memory_space=pltpu.VMEM)
     smem = pl.BlockSpec(memory_space=pltpu.SMEM)
     dma = pltpu.SemaphoreType.DMA
@@ -341,11 +318,9 @@
         scratch_shapes=[
             pltpu.VMEM((vl * pts, local), F32),
             pltpu.VMEM((vl * pts, local), F32),
-            pltpu.VMEM(((faces + 1) * pts, 4 * pts), BF16),
-            pltpu.VMEM((vl * 2 * pts, 2 * faces * blk), BF16),
-            pltpu.VMEM((vl * 2 * pts, 2 * faces * lane), BF16),
-            pltpu.VMEM((2, faces * blk, blk), BF16),
-            pltpu.VMEM((2, faces * lane, blk), BF16),
+            pltpu.VMEM((vl * pts, local), F32),
+            pltpu.VMEM((2 * pts, 2 * (faces + 1) * pts), BF16),
+            pltpu.VMEM((4, 2 * lane, faces * lane), BF16),
             pltpu.VMEM((3, 2, half, lane), F32),
             pltpu.VMEM((3, 2, half, lane), F32),
             pltpu.VMEM((2, slips + 1, pts, lane), F32),

time: 84.2 us -> 80.2 us (0.952)
  the two profiles are of different devices: /device:TPU:16 before, /device:TPU:21 now
where the time goes in v2:
time: 80.2 us; the launch traced here: 80 us
  Pallas kernels  73.4 us (92%)
  local copies, waits for them, and re-layouts  5.59 us (7%)
  other arithmetic  0.96 us (1%)
    pallas_call x1, Pallas kernels, per_device(): pl.pallas_call(functools.partial(kernel, (zones_n, chips_n, vl, pts, loca...  73.4 us
    unnamed x2, local copies, waits for them, and re-layouts  4.05 us

profile of v2, /device:TPU:21, one launch (start us, length us, event | category | flops | bytes accessed | tf_op | source)
XLA Modules:
  0.0 80.0 jit_solution(13851840362638286399)
XLA Ops:
  0.0 1.4 %copy.8.schmid_ref = f32[48,12]{1,0:T(8,128)} copy(f32[48,12]{0,1:T(8,128)} %param.10) | data formatting | bytes 4608 | tf_op args[4]
  1.4 1.0 %pad_maximum_fusion = f32[7,64,64]{2,1,0:T(8,128)S(1)} fusion(f32[1,64,64]{2,1,0:T(8,128)} %bitcast.9, f32[6,64,64]{2,1,0:T(8,128)} %param.9), kind=kLoop, calls=%fused_computation | loop fusion | flops 28672 | bytes 229376 | tf_op jit(solution)/shard_map/concatenate | solution.py:308
  2.3 0.1 copy.7
  2.5 0.1 tile.4
  2.6 1.3 %tile.10.op_ref = f32[128,896]{1,0:T(8,128)} reshape(f32[2,64,2,448]{3,2,1,0:T(2,128)S(1)} %tile.4) | data formatting | bytes 917504 | tf_op jit(solution)/shard_map/tile | solution.py:309
  3.9 73.4 %shard_map.64 = f32[768,512]{1,0:T(8,128)} custom-call(s32[6,512]{1,0:T(8,128)} %adj_ref.1, f32[128,896]{1,0:T(8,128)} %tile.10.op_ref, f32[48,12]{1,0:T(8,128)} %copy.8.schmid_ref, f32[12,48]{1,0:T(8,128)} %hard_ref.1, f32[768,512]{1,0:T(8,128)} %bitcast.7), custom_call_target="tpu_custom_call" | custom-call | tf_op jit(solution)/shard_map/pallas_call | solution.py:313
  77.3 2.7 %copy.10 = f32[12,64,512]{2,1,0:T(8,128)} copy(f32[12,64,512]{2,1,0:T(8,128)} %bitcast.6) | data formatting | bytes 3145728

commit v3 on v2

--- a/solution.py
+++ b/solution.py
@@ -163,7 +163,7 @@
                     total = h_ref[rows, cols] * (1.0 / 3.0) + (2.0 / 3.0) * total
                 dst[rows, cols] = total
             return 0
-        lax.fori_loop(0, vl // 2, body, 0, unroll=3 if vl % 6 == 0 else 1)
+        lax.fori_loop(0, vl // 2, body, 0, unroll=vl // 2)
 
     def shear_chunk(col, dest, rot_row):
         def body(t, _):

time: 80.2 us -> 75 us (0.935)
  the two profiles are of different devices: /device:TPU:21 before, /device:TPU:16 now
where the time goes in v3:
time: 75 us; the launch traced here: 73.6 us
  Pallas kernels  67 us (89%)
  local copies, waits for them, and re-layouts  5.59 us (7%)
  other arithmetic  0.96 us (1%)
    pallas_call x1, Pallas kernels, per_device(): pl.pallas_call(functools.partial(kernel, (zones_n, chips_n, vl, pts, loca...  67 us
    unnamed x2, local copies, waits for them, and re-layouts  4.05 us

profile of v3, /device:TPU:16, one launch (start us, length us, event | category | flops | bytes accessed | tf_op | source)
XLA Modules:
  0.0 73.6 jit_solution(13429536673680728809)
XLA Ops:
  0.0 1.4 %copy.8.schmid_ref = f32[48,12]{1,0:T(8,128)} copy(f32[48,12]{0,1:T(8,128)} %param.10) | data formatting | bytes 4608 | tf_op args[4]
  1.4 1.0 %pad_maximum_fusion = f32[7,64,64]{2,1,0:T(8,128)S(1)} fusion(f32[1,64,64]{2,1,0:T(8,128)} %bitcast.9, f32[6,64,64]{2,1,0:T(8,128)} %param.9), kind=kLoop, calls=%fused_computation | loop fusion | flops 28672 | bytes 229376 | tf_op jit(solution)/shard_map/concatenate | solution.py:308
  2.3 0.1 copy.7
  2.5 0.1 tile.4
  2.6 1.3 %tile.10.op_ref = f32[128,896]{1,0:T(8,128)} reshape(f32[2,64,2,448]{3,2,1,0:T(2,128)S(1)} %tile.4) | data formatting | bytes 917504 | tf_op jit(solution)/shard_map/tile | solution.py:309
  3.9 67.0 %shard_map.64 = f32[768,512]{1,0:T(8,128)} custom-call(s32[6,512]{1,0:T(8,128)} %adj_ref.1, f32[128,896]{1,0:T(8,128)} %tile.10.op_ref, f32[48,12]{1,0:T(8,128)} %copy.8.schmid_ref, f32[12,48]{1,0:T(8,128)} %hard_ref.1, f32[768,512]{1,0:T(8,128)} %bitcast.7), custom_call_target="tpu_custom_call" | custom-call | tf_op jit(solution)/shard_map/pallas_call | solution.py:313
  70.9 2.7 %copy.10 = f32[12,64,512]{2,1,0:T(8,128)} copy(f32[12,64,512]{2,1,0:T(8,128)} %bitcast.6) | data formatting | bytes 3145728
